TPU v7x, 32 devices: a whole 2x2x4 slice. The times are simulated.
32 devices in a mesh: fsdp: 4 (over z), ctx: 4 (over y, x), tp: 2 (over core).
Axes of the slice: x: 2, y: 2, z: 4, core: 2. Of those that a mesh axis runs over, the one named last changes fastest.
Arguments:
- inputs: bfloat16 [4, 1024, 2048], P('fsdp', 'ctx'), may hold values from -6 to 6
- segments: int32 [4, 1024], P('fsdp', 'ctx'), may hold values from 0 to 128, as said below
- positions: int32 [4, 1024], P('fsdp', 'ctx'), may hold values from 0 to 767, as said below
- norm_gain: bfloat16 [2048], P(('fsdp', 'ctx')), may hold values from 0.099609375 to 1.8984375
- query_weight: bfloat16 [2048, 2048], P(('fsdp', 'ctx'), 'tp'), may hold values from -0.125 to 0.125
- key_weight: bfloat16 [2048, 2048], P(('fsdp', 'ctx'), 'tp'), may hold values from -0.125 to 0.125
- value_weight: bfloat16 [2048, 2048], P(('fsdp', 'ctx'), 'tp'), may hold values from -0.125 to 0.125
- out_weight: bfloat16 [2048, 2048], P('tp', ('fsdp', 'ctx')), may hold values from -0.5 to 0.5
- lambdas: float32 [4, 128], replicated, may hold values from -0.8 to 0.8
- head_gain: float32 [256], replicated, may hold values from 0.1 to 1.9
- ffn_gain: bfloat16 [2048], P(('fsdp', 'ctx')), may hold values from 0.099609375 to 1.8984375
- gate_weight: bfloat16 [2048, 5632], P(('fsdp', 'ctx'), 'tp'), may hold values from -0.125 to 0.125
- up_weight: bfloat16 [2048, 5632], P(('fsdp', 'ctx'), 'tp'), may hold values from -0.125 to 0.125
- down_weight: bfloat16 [5632, 2048], P('tp', ('fsdp', 'ctx')), may hold values from -0.078125 to 0.078125
- cotangent: bfloat16 [4, 1024, 2048], P('fsdp', 'ctx'), may hold values from -6 to 6
Outputs:
- output: bfloat16 [4, 1024, 2048], P('fsdp', 'ctx')
- grad_input: bfloat16 [4, 1024, 2048], P('fsdp', 'ctx')
- grad_norm_gain: float32 [2048], P(('fsdp', 'ctx'))
- grad_query: float32 [2048, 2048], P(('fsdp', 'ctx'), 'tp')
- grad_key: float32 [2048, 2048], P(('fsdp', 'ctx'), 'tp')
- grad_value: float32 [2048, 2048], P(('fsdp', 'ctx'), 'tp')
- grad_out: float32 [2048, 2048], P('tp', ('fsdp', 'ctx'))
- grad_lambdas: float32 [4, 128], replicated
- grad_head_gain: float32 [256], replicated
- grad_ffn_gain: float32 [2048], P(('fsdp', 'ctx'))
- grad_gate: float32 [2048, 5632], P(('fsdp', 'ctx'), 'tp')
- grad_up: float32 [2048, 5632], P(('fsdp', 'ctx'), 'tp')
- grad_down: float32 [5632, 2048], P('tp', ('fsdp', 'ctx'))
Inputs may be any that keep to these rules, and one draw needn't show every extreme that they name: `segments`: within a row, document numbers start at 0, never fall along the row, and rise by at most one from a token to the next. `positions`: each token's position within its document: 0 at a document's first token, one more at each further token of it.
All inputs are finite; a program needn't handle non-finite values.
Results may differ from a plain program's by a relative error of at most 0.025.
Values may be sent and summed in bfloat16 or wider, within the bound.
No kernel may reach another device: no remote copies, remote signals or barrier semaphores. Data moves between devices by JAX's collectives and lax.ppermute only.
A program may use at most 256 MiB of HBM per device.

v0:
```python
import math

import jax
import jax.numpy as jnp
from jax import lax
from jax.sharding import PartitionSpec as P

epsilon = 1e-05
rope_base = 10000.0
lambda_init = 0.8 - 0.6 * math.exp(-1.8)
masked_score = -1e30


def cut_along(array, dim, count):
    before, after = (array.shape[:dim], array.shape[dim + 1 :])
    return jnp.moveaxis(array.reshape(*before, count, -1, *after), dim, 0)


def sum_at_owner(array, axis, dim):
    blocks = cut_along(array, dim, lax.axis_size(axis))
    arrived = lax.all_to_all(blocks, axis, split_axis=0, concat_axis=0, tiled=True)
    return arrived.astype(jnp.float32).sum(axis=0)


def side_by_side(arrays, axis, dim, along):
    columns = [a.reshape(*a.shape[:along], -1) for a in arrays]
    both = jnp.concatenate(columns, axis=along)
    whole, at, finished = (sum_at_owner(both, axis, dim), 0, [])
    for a, column in zip(arrays, columns):
        slab = whole[..., at : at + column.shape[along]]
        finished.append(slab.reshape(*slab.shape[:along], *a.shape[along:]))
        at += column.shape[along]
    return tuple(finished)


def rotary_tables(positions, width):
    halfway = width // 2
    spacing = jnp.arange(halfway, dtype=jnp.float32) * (2.0 / width)
    frequency = jnp.exp(-math.log(rope_base) * spacing)
    angles = positions.astype(jnp.float32)[..., None] * frequency
    cosine = jnp.concatenate([jnp.cos(angles), jnp.cos(angles)], axis=-1)
    sine_table = jnp.concatenate([jnp.sin(angles), jnp.sin(angles)], axis=-1)
    return (cosine[:, None, None, :], sine_table[:, None, None, :])


def rotate(values, cosine, sine_table):
    halfway = values.shape[-1] // 2
    turned = jnp.concatenate([-values[..., halfway:], values[..., :halfway]], axis=-1)
    return values * cosine + turned * sine_table


def normalize(values):
    inverse = lax.rsqrt(jnp.mean(values * values, axis=-1, keepdims=True) + epsilon)
    return (values * inverse, inverse)


def normalize_back(grad_unit, unit_rows, inverse):
    return inverse * (
        grad_unit - unit_rows * jnp.mean(grad_unit * unit_rows, axis=-1, keepdims=True)
    )


def tensor_total(part_sum):
    return lax.psum(part_sum, "tp")


def fetch_attention(norm_gain, query_weight, key_weight, value_weight, out_weight):
    row_parts = (
        lax.all_gather(norm_gain, ("fsdp", "ctx"), axis=0, tiled=True),
        lax.all_gather(query_weight, ("fsdp", "ctx"), axis=0, tiled=True),
        lax.all_gather(key_weight, ("fsdp", "ctx"), axis=0, tiled=True),
        lax.all_gather(value_weight, ("fsdp", "ctx"), axis=0, tiled=True),
    )
    columns = lax.all_gather(out_weight, ("fsdp", "ctx"), axis=1, tiled=True)
    return (row_parts, columns)


def fetch_ffn(ffn_gain, gate_weight, up_weight, down_weight):
    row_parts = (
        lax.all_gather(ffn_gain, ("fsdp", "ctx"), axis=0, tiled=True),
        lax.all_gather(gate_weight, ("fsdp", "ctx"), axis=0, tiled=True),
        lax.all_gather(up_weight, ("fsdp", "ctx"), axis=0, tiled=True),
    )
    columns = lax.all_gather(down_weight, ("fsdp", "ctx"), axis=1, tiled=True)
    return (row_parts, columns)


def shards(
    inputs,
    segments,
    positions,
    norm_gain,
    query_weight,
    key_weight,
    value_weight,
    out_weight,
    lambdas,
    head_gain,
    ffn_gain,
    gate_weight,
    up_weight,
    down_weight,
    cotangent,
):
    token_count = inputs.shape[1]
    qk_width = lambdas.shape[1]
    value_width = head_gain.shape[0]
    heads_here = value_weight.shape[1] // value_width
    length = token_count * lax.axis_size("ctx")
    block_rows = min(512, length)
    block_count = length // block_rows
    scaling = 1.0 / math.sqrt(qk_width)
    query_places = lax.axis_index("ctx") * token_count + jnp.arange(token_count, dtype=jnp.int32)
    query_seg = segments[0]
    cosine, sine_table = rotary_tables(positions[0], qk_width)
    hidden_in = inputs[0].astype(jnp.float32)
    unit_one, inverse_one = normalize(hidden_in)
    attn_parts, out_full = fetch_attention(
        norm_gain, query_weight, key_weight, value_weight, out_weight
    )
    gain_one, query_full, key_full, value_full = attn_parts
    normed_one = (unit_one * gain_one.astype(jnp.float32)).astype(jnp.bfloat16)
    query_pre = jnp.dot(normed_one, query_full, preferred_element_type=jnp.float32).reshape(
        token_count, heads_here, 2, qk_width
    )
    key_pre = jnp.dot(normed_one, key_full, preferred_element_type=jnp.float32).reshape(
        token_count, heads_here, 2, qk_width
    )
    value_rows = (
        jnp.dot(normed_one, value_full, preferred_element_type=jnp.float32)
        .astype(jnp.bfloat16)
        .reshape(token_count, heads_here, value_width)
    )
    query_rot = rotate(query_pre, cosine, sine_table).astype(jnp.bfloat16)
    key_rot = rotate(key_pre, cosine, sine_table).astype(jnp.bfloat16)
    first_exp = jnp.exp(jnp.sum(lambdas[0] * lambdas[1]))
    second_exp = jnp.exp(jnp.sum(lambdas[2] * lambdas[3]))
    weight_lambda = first_exp - second_exp + lambda_init
    seg_all = lax.all_gather(query_seg, "ctx", axis=0, tiled=True)
    keys_all, values_all = (
        lax.all_gather(key_rot, "ctx", axis=0, tiled=True),
        lax.all_gather(value_rows, "ctx", axis=0, tiled=True),
    )
    all_places = jnp.arange(length, dtype=jnp.int32)
    blocks = (
        keys_all.reshape(block_count, block_rows, heads_here, 2, qk_width),
        values_all.reshape(block_count, block_rows, heads_here, value_width),
        seg_all.reshape(block_count, block_rows),
        all_places.reshape(block_count, block_rows),
    )

    def block_scores(block):
        scores = (
            jnp.einsum("thmd,khmd->hmtk", query_rot, block[0], preferred_element_type=jnp.float32)
            * scaling
        )
        allowed = (query_seg[:, None] == block[2][None, :]) & (
            block[3][None, :] <= query_places[:, None]
        )
        allowed = allowed[None, None]
        return (jnp.where(allowed, scores, masked_score), allowed)

    def stats_step(carry, block):
        largest, total = carry
        masked, allowed = block_scores(block)
        fresh = jnp.maximum(largest, jnp.max(masked, axis=-1))
        total = total * jnp.exp(largest - fresh) + jnp.sum(
            jnp.where(allowed, jnp.exp(masked - fresh[..., None]), 0.0), axis=-1
        )
        return ((fresh, total), None)

    start_max = jnp.full((heads_here, 2, token_count), masked_score, jnp.float32)
    (largest, total), unused = lax.scan(stats_step, (start_max, jnp.zeros_like(start_max)), blocks)
    log_total = largest + jnp.log(total)

    def block_shares(block):
        masked, allowed = block_scores(block)
        shares = jnp.where(allowed, jnp.exp(masked - log_total[..., None]), 0.0)
        mix = (shares[:, 0] - weight_lambda * shares[:, 1]).astype(jnp.bfloat16)
        return (shares, mix)

    def output_step(attended, block):
        shares, mix = block_shares(block)
        return (
            attended
            + jnp.einsum("htk,khv->thv", mix, block[1], preferred_element_type=jnp.float32),
            None,
        )

    attended, unused = lax.scan(
        output_step, jnp.zeros((token_count, heads_here, value_width), jnp.float32), blocks
    )
    unit_head, inverse_head = normalize(attended)
    headed = (
        (unit_head * head_gain * (1.0 - lambda_init))
        .astype(jnp.bfloat16)
        .reshape(token_count, heads_here * value_width)
    )
    middle = hidden_in + tensor_total(jnp.dot(headed, out_full, preferred_element_type=jnp.float32))
    ffn_parts, down_full = fetch_ffn(ffn_gain, gate_weight, up_weight, down_weight)
    gain_two, gate_full, up_full = ffn_parts
    unit_two, inverse_two = normalize(middle)
    normed_two = (unit_two * gain_two.astype(jnp.float32)).astype(jnp.bfloat16)
    gate_rows = jnp.dot(normed_two, gate_full, preferred_element_type=jnp.float32)
    upward = jnp.dot(normed_two, up_full, preferred_element_type=jnp.float32)
    hidden_units = (jax.nn.silu(gate_rows) * upward).astype(jnp.bfloat16)
    result = middle + tensor_total(
        jnp.dot(hidden_units, down_full, preferred_element_type=jnp.float32)
    )
    ffn_parts, down_full = fetch_ffn(ffn_gain, gate_weight, up_weight, down_weight)
    gain_two, gate_full, up_full = ffn_parts
    grad_rows = cotangent[0]
    grad_down_full = jnp.einsum(
        "tf,td->fd", hidden_units, grad_rows, preferred_element_type=jnp.float32
    )
    hidden_grad = jnp.einsum("td,fd->tf", grad_rows, down_full, preferred_element_type=jnp.float32)
    sigmoid = jax.nn.sigmoid(gate_rows)
    gate_low = (hidden_grad * upward * (sigmoid * (1.0 + gate_rows * (1.0 - sigmoid)))).astype(
        jnp.bfloat16
    )
    up_low = (hidden_grad * (gate_rows * sigmoid)).astype(jnp.bfloat16)
    grad_gate_full = jnp.einsum(
        "td,tf->df", normed_two, gate_low, preferred_element_type=jnp.float32
    )
    grad_up_full = jnp.einsum("td,tf->df", normed_two, up_low, preferred_element_type=jnp.float32)
    normed_two_grad = tensor_total(
        jnp.einsum("tf,df->td", gate_low, gate_full, preferred_element_type=jnp.float32)
        + jnp.einsum("tf,df->td", up_low, up_full, preferred_element_type=jnp.float32)
    )
    gain_two_grad = jnp.sum(normed_two_grad * unit_two, axis=0)
    middle_grad = grad_rows.astype(jnp.float32) + normalize_back(
        normed_two_grad * gain_two.astype(jnp.float32), unit_two, inverse_two
    )
    grad_ffn_gain, grad_gate, grad_up = (
        lax.psum_scatter(gain_two_grad, ("fsdp", "ctx"), scatter_dimension=0, tiled=True),
        lax.psum_scatter(grad_gate_full, ("fsdp", "ctx"), scatter_dimension=0, tiled=True),
        lax.psum_scatter(grad_up_full, ("fsdp", "ctx"), scatter_dimension=0, tiled=True),
    )
    grad_down = lax.psum_scatter(grad_down_full, ("fsdp", "ctx"), scatter_dimension=1, tiled=True)
    attn_parts, out_full = fetch_attention(
        norm_gain, query_weight, key_weight, value_weight, out_weight
    )
    gain_one, query_full, key_full, value_full = attn_parts
    branch_grad = middle_grad.astype(jnp.bfloat16)
    grad_out_full = jnp.einsum("tf,td->fd", headed, branch_grad, preferred_element_type=jnp.float32)
    headed_grad = jnp.einsum(
        "td,fd->tf", branch_grad, out_full, preferred_element_type=jnp.float32
    ).reshape(token_count, heads_here, value_width)
    scaled_grad = headed_grad * (1.0 - lambda_init)
    head_gain_grad = jnp.sum(scaled_grad * unit_head, axis=(0, 1))
    attended_grad = normalize_back(scaled_grad * head_gain, unit_head, inverse_head).astype(
        jnp.bfloat16
    )

    def sums_step(carry, block):
        first_sum, second_sum = carry
        shares, mix = block_shares(block)
        mix_grad = jnp.einsum(
            "thv,khv->htk", attended_grad, block[1], preferred_element_type=jnp.float32
        )
        return (
            (
                first_sum + jnp.sum(shares[:, 0] * mix_grad, axis=-1),
                second_sum + jnp.sum(shares[:, 1] * mix_grad, axis=-1),
            ),
            None,
        )

    start_sums = jnp.zeros((heads_here, token_count), jnp.float32)
    (first_sum, second_sum), unused = lax.scan(sums_step, (start_sums, start_sums), blocks)
    query_start = jnp.zeros((token_count, heads_here, 2, qk_width), jnp.float32)

    def grad_step(query_grad, block):
        shares, mix = block_shares(block)
        mix_grad = jnp.einsum(
            "thv,khv->htk", attended_grad, block[1], preferred_element_type=jnp.float32
        )
        score_grad = jnp.stack(
            [
                shares[:, 0] * (mix_grad - first_sum[..., None]),
                -weight_lambda * shares[:, 1] * (mix_grad - second_sum[..., None]),
            ],
            axis=1,
        ).astype(jnp.bfloat16)
        query_grad = query_grad + jnp.einsum(
            "hmtk,khmd->thmd", score_grad, block[0], preferred_element_type=jnp.float32
        )
        key_block_grad = (
            jnp.einsum("hmtk,thmd->khmd", score_grad, query_rot, preferred_element_type=jnp.float32)
            * scaling
        )
        value_block_grad = jnp.einsum(
            "htk,thv->khv", mix, attended_grad, preferred_element_type=jnp.float32
        )
        return (query_grad, (key_block_grad, value_block_grad))

    query_grad, (key_stack, value_stack) = lax.scan(grad_step, query_start, blocks)
    key_back, value_back = (
        lax.psum_scatter(
            key_stack.reshape(length, heads_here, 2, qk_width),
            "ctx",
            scatter_dimension=0,
            tiled=True,
        ),
        lax.psum_scatter(
            value_stack.reshape(length, heads_here, value_width),
            "ctx",
            scatter_dimension=0,
            tiled=True,
        ),
    )
    query_low = (
        rotate(query_grad * scaling, cosine, -sine_table)
        .astype(jnp.bfloat16)
        .reshape(token_count, heads_here * 2 * qk_width)
    )
    key_low = (
        rotate(key_back, cosine, -sine_table)
        .astype(jnp.bfloat16)
        .reshape(token_count, heads_here * 2 * qk_width)
    )
    value_low = value_back.astype(jnp.bfloat16).reshape(token_count, heads_here * value_width)
    grad_query_full = jnp.einsum(
        "td,tf->df", normed_one, query_low, preferred_element_type=jnp.float32
    )
    grad_key_full = jnp.einsum("td,tf->df", normed_one, key_low, preferred_element_type=jnp.float32)
    grad_value_full = jnp.einsum(
        "td,tf->df", normed_one, value_low, preferred_element_type=jnp.float32
    )
    normed_one_part = jnp.einsum(
        "tf,df->td", query_low, query_full, preferred_element_type=jnp.float32
    )
    normed_one_part = normed_one_part + jnp.einsum(
        "tf,df->td", key_low, key_full, preferred_element_type=jnp.float32
    )
    normed_one_part = normed_one_part + jnp.einsum(
        "tf,df->td", value_low, value_full, preferred_element_type=jnp.float32
    )
    normed_one_grad = tensor_total(normed_one_part)
    gain_one_grad = jnp.sum(normed_one_grad * unit_one, axis=0)
    input_grad = middle_grad + normalize_back(
        normed_one_grad * gain_one.astype(jnp.float32), unit_one, inverse_one
    )
    grad_norm_gain, grad_query, grad_key, grad_value = side_by_side(
        (
            gain_one_grad.astype(jnp.bfloat16),
            grad_query_full.astype(jnp.bfloat16),
            grad_key_full.astype(jnp.bfloat16),
            grad_value_full.astype(jnp.bfloat16),
        ),
        ("fsdp", "ctx"),
        0,
        1,
    )
    grad_out = lax.psum_scatter(grad_out_full, ("fsdp", "ctx"), scatter_dimension=1, tiled=True)
    lambda_scalar = -jnp.sum(second_sum)
    lambda_local = lambda_scalar * jnp.stack(
        [
            first_exp * lambdas[1],
            first_exp * lambdas[0],
            -second_exp * lambdas[3],
            -second_exp * lambdas[2],
        ]
    )
    grad_lambdas, grad_head_gain = lax.psum((lambda_local, head_gain_grad), ("fsdp", "ctx", "tp"))
    return (
        result.astype(jnp.bfloat16)[None],
        input_grad.astype(jnp.bfloat16)[None],
        grad_norm_gain,
        grad_query,
        grad_key,
        grad_value,
        grad_out,
        grad_lambdas,
        grad_head_gain,
        grad_ffn_gain,
        grad_gate,
        grad_up,
        grad_down,
    )


def solution(mesh):
    placed = (
        P("fsdp", "ctx", None),
        P("fsdp", "ctx"),
        P("fsdp", "ctx"),
        P(("fsdp", "ctx")),
        P(("fsdp", "ctx"), "tp"),
        P(("fsdp", "ctx"), "tp"),
        P(("fsdp", "ctx"), "tp"),
        P("tp", ("fsdp", "ctx")),
        P(),
        P(),
        P(("fsdp", "ctx")),
        P(("fsdp", "ctx"), "tp"),
        P(("fsdp", "ctx"), "tp"),
        P("tp", ("fsdp", "ctx")),
        P("fsdp", "ctx", None),
    )
    return jax.shard_map(
        shards,
        mesh=mesh,
        in_specs=placed,
        out_specs=(
            P("fsdp", "ctx", None),
            P("fsdp", "ctx", None),
            P(("fsdp", "ctx")),
            P(("fsdp", "ctx"), "tp"),
            P(("fsdp", "ctx"), "tp"),
            P(("fsdp", "ctx"), "tp"),
            P("tp", ("fsdp", "ctx")),
            P(),
            P(),
            P(("fsdp", "ctx")),
            P(("fsdp", "ctx"), "tp"),
            P(("fsdp", "ctx"), "tp"),
            P("tp", ("fsdp", "ctx")),
        ),
        check_vma=False,
    )
```

profile of v0, /device:TPU:10, one launch (start us, length us, event | category | flops | bytes accessed | tf_op | source)
XLA Modules:
  0.0 3113.9 jit_solution(12823206344899323226)
XLA Ops:
  9.5 29.9 all-gather.1
  41.5 46.3 %all-gather.21.cloned.1.call-done = bf16[2048,1024]{1,0:T(8,128)(2,1)} async-done(((bf16[128,1024]{1,0:T(8,128)(2,1)}), bf16[2048,1024]{1,0:T(8,128)(2,1)}) %all-gather.21.cloned.1.call-update) | async-done | bytes 4194320 | tf_op jit(solution)/shard_map/all_gather | solution.py:70
  94.3 71.0 %all-gather.17.cloned.1.call-done = bf16[2048,1024]{1,0:T(8,128)(2,1)} async-done(((bf16[128,1024]{1,0:T(8,128)(2,1)}), bf16[2048,1024]{1,0:T(8,128)(2,1)}) %all-gather.17.cloned.1.call-update) | async-done | bytes 4194320 | tf_op jit(solution)/shard_map/all_gather | solution.py:71
  178.4 64.4 %all-gather.13.cloned.1.call-done = bf16[2048,1024]{1,0:T(8,128)(2,1)} async-done(((bf16[128,1024]{1,0:T(8,128)(2,1)}), bf16[2048,1024]{1,0:T(8,128)(2,1)}) %all-gather.13.cloned.1.call-update) | async-done | bytes 4194320 | tf_op jit(solution)/shard_map/all_gather | solution.py:72
  258.6 20.2 all-gather.19.cloned.1.call-done
  289.5 14.9 while.53
  316.5 16.2 while.54
  332.9 72.5 %all-gather.23.cloned.1.call-done = bf16[1024,2048]{1,0:T(8,128)(2,1)} async-done(((bf16[1024,128]{1,0:T(8,128)(2,1)}), bf16[1024,2048]{1,0:T(8,128)(2,1)}) %all-gather.23.cloned.1.call-update) | async-done | bytes 4194320 | tf_op jit(solution)/shard_map/all_gather | solution.py:74
  412.3 32.6 %all-gather.2 = bf16[16,1,128]{2,1,0:T(2,128)(2,1)S(1)} all-gather(bf16[1,1,128]{2,1,0:T(2,128)(2,1)S(1)} %bitcast.434), channel_id=1, replica_groups=mesh['fsdp'=4,'ctx'=4,'tp'=2] {'fsdp','ctx'}, dimensions={0}, use_global_device_ids=true | all-gather | bytes 4352 | tf_op jit(solution)/shard_map/all_gather | solution.py:80
  448.7 128.3 %all-gather.25.cloned.1.call-done = bf16[2048,2816]{1,0:T(8,128)(2,1)} async-done(((bf16[128,2816]{1,0:T(8,128)(2,1)}), bf16[2048,2816]{1,0:T(8,128)(2,1)}) %all-gather.25.cloned.1.call-update) | async-done | bytes 11534352 | tf_op jit(solution)/shard_map/all_gather | solution.py:81
  586.0 134.5 %all-gather.27.cloned.1.call-done = bf16[2048,2816]{1,0:T(8,128)(2,1)} async-done(((bf16[128,2816]{1,0:T(8,128)(2,1)}), bf16[2048,2816]{1,0:T(8,128)(2,1)}) %all-gather.27.cloned.1.call-update) | async-done | bytes 11534352 | tf_op jit(solution)/shard_map/all_gather | solution.py:82
  729.5 173.9 %all-gather.29.cloned.1.call-done = bf16[2816,2048]{1,0:T(8,128)(2,1)} async-done(((bf16[2816,128]{1,0:T(8,128)(2,1)}), bf16[2816,2048]{1,0:T(8,128)(2,1)}) %all-gather.29.cloned.1.call-update) | async-done | bytes 11534352 | tf_op jit(solution)/shard_map/all_gather | solution.py:84
  934.1 19.4 all-reduce.9.cloned.1.call-done
  969.0 115.8 %while.56 = (s32[]{:T(128)}, f32[256,4,2,128]{0,3,2,1:T(8,128)}, f32[2,512,4,2,128]{1,0,4,3,2:T(2,128)}, f32[2,512,4,256]{3,1,0,2:T(8,128)}, bf16[2,512,4,2,128]...) while((s32[]{:T(128)}, f32[256,4,2,128]{0,3,2,1:T(8,128)}, ...), condition=%wide.region_21.22_spmd.clone, body=%wide.region_20.21_spmd.clone.sunk | while | flops 1355153664 | bytes 81036656 | solution.py:297
  981.8 38.1 %dynamic_update_slice.16 = f32[2,512,4,2,128]{1,0,4,3,2:T(2,128)} dynamic-update-slice(f32[2,512,4,2,128]{1,0,4,3,2:T(2,128)} %get-tuple-element.1390, f32[1,512,4,2,128]{1,0,4,3,2:T(1,128)S(1)} %copy.218, s32[]{:T(128)} %get-tuple-element.1388, s32[]{:T(128)} %constant.110.clone.1..sunk.3, s32[]{:T(128)} %constant.110.clone.1..sunk.3, s32[]{:T(128)} %constant.110.clone.1..sunk.3, ...) | dynamic-update-slice | bytes 4194308 | tf_op jit(solution)/shard_map/while/body/jit(dynamic_update_index_in_dim)/dynamic_update_slice | solution.py:297
  1039.5 38.1 %dynamic_update_slice.16 = f32[2,512,4,2,128]{1,0,4,3,2:T(2,128)} dynamic-update-slice(f32[2,512,4,2,128]{1,0,4,3,2:T(2,128)} %get-tuple-element.1390, f32[1,512,4,2,128]{1,0,4,3,2:T(1,128)S(1)} %copy.218, s32[]{:T(128)} %get-tuple-element.1388, s32[]{:T(128)} %constant.110.clone.1..sunk.3, s32[]{:T(128)} %constant.110.clone.1..sunk.3, s32[]{:T(128)} %constant.110.clone.1..sunk.3, ...) | dynamic-update-slice | bytes 4194308 | tf_op jit(solution)/shard_map/while/body/jit(dynamic_update_index_in_dim)/dynamic_update_slice | solution.py:297
  1103.0 35.4 %reduce-scatter.9.cloned.1.call-done = f32[256,4,256]{2,0,1:T(8,128)} async-done(((f32[1024,4,256]{2,0,1:T(8,128)}), f32[256,4,256]{2,0,1:T(8,128)}) %reduce-scatter.9.cloned.1.call-update) | async-done | bytes 1048592 | tf_op jit(solution)/shard_map/reduce_scatter | solution.py:305
  1139.9 54.4 %reduce-scatter.7.cloned.1.call-done = f32[256,4,2,128]{0,3,2,1:T(8,128)} async-done(((f32[1024,4,2,128]{0,3,2,1:T(8,128)}), f32[256,4,2,128]{0,3,2,1:T(8,128)}) %reduce-scatter.7.cloned.1.call-update) | async-done | bytes 1048592 | tf_op jit(solution)/shard_map/reduce_scatter | solution.py:299
  1283.1 79.9 %concatenate.41 = bf16[16,128,3073]{1,2,0:T(8,128)(2,1)} concatenate(bf16[16,128,1]{1,2,0:T(2,128)(2,1)S(1)} %copy.166, bf16[16,128,1024]{1,2,0:T(8,128)(2,1)} %copy.167, bf16[16,128,1024]{1,2,0:T(8,128)(2,1)} %copy.168, bf16[16,128,1024]{1,2,0:T(8,128)(2,1)} %copy.169), dimensions={2} | concatenate | bytes 25174016 | tf_op jit(solution)/shard_map/concatenate | solution.py:27
  1371.7 435.2 %all-reduce = f32[2048]{0:T(1024)S(1)} all-reduce(f32[2048]{0:T(1024)S(1)} %copy-done.44), channel_id=6, replica_groups=mesh['fsdp'=4,'ctx'=4,'tp'=2] {'fsdp','ctx'}, use_global_device_ids=true, to_apply=%region_34.35.clone | all-reduce | flops 2048 | bytes 16384
  1807.5 60.6 %all-reduce.1 = (f32[4,128]{1,0:T(4,128)}, f32[256]{0:T(256)}) all-reduce(f32[4,128]{1,0:T(4,128)S(1)} %maximum_multiply_fusion.4, f32[256]{0:T(256)S(1)} %copy-done.47), channel_id=1, replica_groups=mesh['fsdp'=4,'ctx'=4,'tp'=2] {'fsdp','ctx','tp'}, use_global_device_ids=true, to_apply=%region_30.31 | all-reduce | flops 768 | bytes 6144 | tf_op jit(solution)/shard_map/psum | solution.py:365
  1882.9 260.2 %reduce-scatter.13.cloned.1.call-done = f32[128,2816]{1,0:T(8,128)} async-done(((f32[2048,2816]{1,0:T(8,128)}), f32[128,2816]{1,0:T(8,128)}) %reduce-scatter.13.cloned.1.call-update) | async-done | bytes 1441808 | tf_op jit(solution)/shard_map/reduce_scatter | solution.py:236
  2143.1 480.8 %reduce-scatter.15.cloned.1.call-done = f32[128,2816]{1,0:T(8,128)} async-done(((f32[2048,2816]{1,0:T(8,128)}), f32[128,2816]{1,0:T(8,128)}) %reduce-scatter.15.cloned.1.call-update) | async-done | bytes 1441808 | tf_op jit(solution)/shard_map/reduce_scatter | solution.py:237
  2623.9 482.7 %reduce-scatter.17.cloned.1.call-done = f32[2816,128]{1,0:T(8,128)} async-done(((f32[2816,2048]{1,0:T(8,128)}), f32[2816,128]{1,0:T(8,128)}) %reduce-scatter.17.cloned.1.call-update) | async-done | bytes 1441808 | tf_op jit(solution)/shard_map/reduce_scatter | solution.py:239
  (312 shorter events, 344.0 us)
Async XLA Ops:
  7.2 80.6 %all-gather.21.cloned.1.call-start = ((), (), s32[]{:S(2)}) async-start(), calls=%async_computation.11 | async-start | bytes 4456448 | tf_op jit(solution)/shard_map/all_gather | solution.py:70
  7.9 157.3 %all-gather.17.cloned.1.call-start = ((), (), s32[]{:S(2)}) async-start(), calls=%async_computation.9 | async-start | bytes 4456448 | tf_op jit(solution)/shard_map/all_gather | solution.py:71
  8.7 234.1 %all-gather.13.cloned.1.call-start = ((), (), s32[]{:S(2)}) async-start(), calls=%async_computation.7 | async-start | bytes 4456448 | tf_op jit(solution)/shard_map/all_gather | solution.py:72
  9.4 269.4 %all-gather.19.cloned.1.call-start = ((), (), s32[]{:S(2)}) async-start(), calls=%async_computation.10 | async-start | bytes 2621440 | tf_op jit(solution)/shard_map/all_gather | solution.py:141
  39.4 203.4 %copy-start.35 = (f32[16,1,128]{2,1,0:T(1,128)}, f32[16,1,128]{2,1,0:T(1,128)S(1)}, u32[]{:S(2)}) copy-start(f32[16,1,128]{2,1,0:T(1,128)S(1)} %convert_element_type.162) | copy-start | bytes 24580
  41.4 201.3 %copy-start.42 = (f32[256]{0:T(256)}, f32[256]{0:T(256)S(1)}, u32[]{:S(2)}) copy-start(f32[256]{0:T(256)S(1)} %add_rsqrt_fusion.2) | copy-start | bytes 3076
  178.3 138.1 %all-gather.15.cloned.1.call-start = ((), (), s32[]{:S(2)}) async-start(), calls=%async_computation.8 | async-start | bytes 2621440 | tf_op jit(solution)/shard_map/all_gather | solution.py:142
  247.1 158.3 %all-gather.23.cloned.1.call-start = ((), (), s32[]{:S(2)}) async-start(), calls=%async_computation.12 | async-start | bytes 4456448 | tf_op jit(solution)/shard_map/all_gather | solution.py:74
  247.7 197.2 %all-reduce.7.cloned.1.call-start = ((), (), s32[]{:S(2)}) async-start(), calls=%async_computation.13 | async-start | bytes 4194304 | tf_op jit(solution)/shard_map/psum | solution.py:64
  410.2 166.8 %all-gather.25.cloned.1.call-start = ((), (), s32[]{:S(2)}) async-start(), calls=%async_computation.14 | async-start | bytes 12255232 | tf_op jit(solution)/shard_map/all_gather | solution.py:81
  410.9 309.6 %all-gather.27.cloned.1.call-start = ((), (), s32[]{:S(2)}) async-start(), calls=%async_computation.15 | async-start | bytes 12255232 | tf_op jit(solution)/shard_map/all_gather | solution.py:82
  411.7 491.8 %all-gather.29.cloned.1.call-start = ((), (), s32[]{:S(2)}) async-start(), calls=%async_computation.16 | async-start | bytes 12255232 | tf_op jit(solution)/shard_map/all_gather | solution.py:84
  412.2 541.2 %all-reduce.9.cloned.1.call-start = ((), (), s32[]{:S(2)}) async-start(), calls=%async_computation.17 | async-start | bytes 4194304 | tf_op jit(solution)/shard_map/psum | solution.py:64
  448.7 271.8 %copy-start.16 = (bf16[256,2048]{1,0:T(8,128)(2,1)}, bf16[256,2048]{1,0:T(8,128)(2,1)S(1)}, u32[]{:S(2)}) copy-start(bf16[256,2048]{1,0:T(8,128)(2,1)S(1)} %multiply_convert_fusion.3) | copy-start | bytes 3145732
  930.8 207.6 %reduce-scatter.9.cloned.1.call-start = ((), (), s32[]{:S(2)}) async-start(), calls=%async_computation.19 | async-start | bytes 5242880 | tf_op jit(solution)/shard_map/reduce_scatter | solution.py:305
  1084.8 109.6 %reduce-scatter.7.cloned.1.call-start = ((), (), s32[]{:S(2)}) async-start(), calls=%async_computation.18 | async-start | bytes 5242880 | tf_op jit(solution)/shard_map/reduce_scatter | solution.py:299
  1091.5 189.3 %all-reduce.11.cloned.1.call-start = ((), (), s32[]{:S(2)}) async-start(), calls=%async_computation.24 | async-start | bytes 8388608 | tf_op jit(solution)/shard_map/psum | solution.py:64
  1205.6 677.3 %reduce-scatter.11.cloned.1.call-start = ((), (), s32[]{:S(2)}) async-start(), calls=%async_computation.20 | async-start | bytes 8912896 | tf_op jit(solution)/shard_map/reduce_scatter | solution.py:355
  1213.0 930.1 %reduce-scatter.13.cloned.1.call-start = ((), (), s32[]{:S(2)}) async-start(), calls=%async_computation.21 | async-start | bytes 24510464 | tf_op jit(solution)/shard_map/reduce_scatter | solution.py:236
  1225.6 1398.4 %reduce-scatter.15.cloned.1.call-start = ((), (), s32[]{:S(2)}) async-start(), calls=%async_computation.22 | async-start | bytes 24510464 | tf_op jit(solution)/shard_map/reduce_scatter | solution.py:237
  1237.4 1869.2 %reduce-scatter.17.cloned.1.call-start = ((), (), s32[]{:S(2)}) async-start(), calls=%async_computation.23 | async-start | bytes 24510464 | tf_op jit(solution)/shard_map/reduce_scatter | solution.py:239
  1363.0 444.5 %copy-start.47 = (f32[256]{0:T(256)S(1)}, f32[256]{0:T(256)}, u32[]{:S(2)}) copy-start(f32[256]{0:T(256)} %get-tuple-element.777) | copy-start | bytes 3076
  1363.0 505.1 %copy-start.5 = (f32[256,2048]{1,0:T(8,128)S(1)}, f32[256,2048]{1,0:T(8,128)}, u32[]{:S(2)}) copy-start(f32[256,2048]{1,0:T(8,128)} %copy-done.3) | copy-start | bytes 6291460
  1363.0 509.7 %all-to-all-start = ((bf16[16,128,3073]{1,2,0:T(8,128)(2,1)}), bf16[16,128,3073]{1,2,0:T(8,128)(2,1)}, u32[]{:S(2)}, u32[]{:S(2)}) async-start(bf16[16,128,3073]{1,2,0:T(8,128)(2,1)} %concatenate.41), calls=%async_computation.2 | async-start | bytes 25231360 | tf_op jit(solution)/shard_map/all_to_all | solution.py:21
  (54 other events, 846.1 us)
Sparse Core Ops, SparseCore 0:
  10.8 76.9 all-gather.20
  90.5 74.6 all-gather.16
  168.0 74.6 all-gather.12
  245.0 33.7 all-gather.18
  281.1 35.3 all-gather.14
  319.0 86.3 all-gather.22
  410.3 22.4 all-reduce.6
  435.9 141.0 all-gather.24
  580.1 140.3 all-gather.26
  723.4 179.9 all-gather.28
  930.9 22.4 all-reduce.8
  1084.9 53.4 reduce-scatter.8
  1141.7 52.6 reduce-scatter.6
  1205.7 28.8 all-reduce.10
  1237.5 227.0 reduce-scatter.10
  1467.4 675.6 reduce-scatter.12
  2145.9 477.9 reduce-scatter.14
  2626.7 479.7 reduce-scatter.16
where the time goes:
time: 3130 us; the launch traced here: 3110 us
  waiting for transfers between devices  2060 us (66%)
  blocking collectives  566 us (18%)
  local copies, waits for them, and re-layouts  244 us (8%)
  matrix products  179 us (6%)
  other arithmetic  39.2 us (1%)
    reduce_scatter x1, waiting for transfers between devices, shards(): lax.psum_scatter(grad_down_full, ('fsdp', 'ctx'), scatter_dimension=1, ti...  483 us
    reduce_scatter x1, waiting for transfers between devices, shards(): lax.psum_scatter(grad_up_full, ('fsdp', 'ctx'), scatter_dimension=0, tile...  481 us
    unnamed x1, blocking collectives  435 us
    reduce_scatter x1, waiting for transfers between devices, shards(): lax.psum_scatter(grad_gate_full, ('fsdp', 'ctx'), scatter_dimension=0, ti...  260 us
    all_gather x1, waiting for transfers between devices, fetch_ffn(): columns = lax.all_gather(down_weight, ('fsdp', 'ctx'), axis=1, tiled=True)  174 us
    all_gather x1, waiting for transfers between devices, fetch_ffn(): lax.all_gather(up_weight, ('fsdp', 'ctx'), axis=0, tiled=True)  134 us
    all_gather x1, waiting for transfers between devices, fetch_ffn(): lax.all_gather(gate_weight, ('fsdp', 'ctx'), axis=0, tiled=True)  128 us
    concatenate x4, local copies, waits for them, and re-layouts, side_by_side(): both = jnp.concatenate(columns, axis=along)  99.1 us
  transfers between devices with their start and end apart: 19, of which 15 were waited for; matrix products, arithmetic and copies ran while one was open for 9% of the time, Pallas kernels for 0%

commit v1 on v0

--- a/solution.py
+++ b/solution.py
@@ -380,6 +380,362 @@
     )
 
 
+heads_total = 8
+
+
+def fits_by_head(sizes):
+    return sizes["ctx"] == 4 and sizes["fsdp"] == 4 and sizes["tp"] == 2
+
+
+def partner(values, axis, step):
+    if step == 0:
+        return values
+    return lax.ppermute(values, axis, [(i, i ^ step) for i in range(lax.axis_size(axis))])
+
+
+def partners(values, axis):
+    return [partner(values, axis, k) for k in range(lax.axis_size(axis))]
+
+
+def reorder(blocks, index):
+    bit = 1
+    while bit < len(blocks):
+        flip = (index & bit) != 0
+        blocks = [jnp.where(flip, blocks[k ^ bit], blocks[k]) for k in range(len(blocks))]
+        bit *= 2
+    return blocks
+
+
+def exchange(blocks, axis):
+    index = lax.axis_index(axis)
+    sent = reorder(blocks, index)
+    return reorder([partner(b, axis, k) for k, b in enumerate(sent)], index)
+
+
+def sum_partners(blocks, axis):
+    total = blocks[0].astype(jnp.float32)
+    for k in range(1, len(blocks)):
+        total = total + partner(blocks[k], axis, k).astype(jnp.float32)
+    return total
+
+
+def split(values, count, dim):
+    return jnp.split(values, count, axis=dim)
+
+
+def gather_tokens(rows, axis):
+    near = jnp.concatenate(partners(rows, axis), axis=0)
+    return jnp.concatenate([near, partner(near, "tp", 1)], axis=0)
+
+
+def scatter_tokens(partial, axis):
+    rows = partial.shape[0] // 2
+    near = partial[:rows].astype(jnp.float32) + partner(partial[rows:], "tp", 1).astype(jnp.float32)
+    return sum_partners(split(near.astype(jnp.bfloat16), lax.axis_size(axis), 0), axis)
+
+
+def times(left, right):
+    return jnp.dot(left, right, preferred_element_type=jnp.float32)
+
+
+def times_t(left, right):
+    return lax.dot_general(left, right, (((1,), (1,)), ((), ())), preferred_element_type=jnp.float32)
+
+
+def t_times(left, right):
+    return lax.dot_general(left, right, (((0,), (0,)), ((), ())), preferred_element_type=jnp.float32)
+
+
+def sum_times(left, rights):
+    parts = split(left, len(rights), 1)
+    total = times(parts[0], rights[0])
+    for a, b in zip(parts[1:], rights[1:]):
+        total = total + times(a, b)
+    return total
+
+
+def by_head(
+    inputs,
+    segments,
+    positions,
+    norm_gain,
+    query_weight,
+    key_weight,
+    value_weight,
+    out_weight,
+    lambdas,
+    head_gain,
+    ffn_gain,
+    gate_weight,
+    up_weight,
+    down_weight,
+    cotangent,
+):
+    token_count, width = inputs.shape[1], inputs.shape[2]
+    half = token_count // 2
+    qk_width = lambdas.shape[1]
+    value_width = head_gain.shape[0]
+    n_z, n_c = lax.axis_size("fsdp"), lax.axis_size("ctx")
+    z, c, core = lax.axis_index("fsdp"), lax.axis_index("ctx"), lax.axis_index("tp")
+    piece = norm_gain.shape[0]
+    scaling = 1.0 / math.sqrt(qk_width)
+    bf16, f32 = jnp.bfloat16, jnp.float32
+
+    def plain_to_near(v):
+        return jnp.concatenate(reorder(split(v, n_z, 1), z), axis=1)
+
+    def plain_to_ffn(v):
+        by_z = [split(b, n_c, 1) for b in split(v, n_z, 1)]
+        by_c = [jnp.concatenate([by_z[i][j] for i in range(n_z)], axis=1) for j in range(n_c)]
+        return jnp.concatenate(reorder(by_c, c), axis=1)
+
+    def ffn_to_plain(v):
+        by_c = [split(b, n_z, 1) for b in reorder(split(v, n_c, 1), c)]
+        return jnp.concatenate(
+            [by_c[j][i] for i in range(n_z) for j in range(n_c)], axis=1
+        )
+
+    def own_half(v):
+        return lax.dynamic_slice_in_dim(v, core * half, half, 0)
+
+    small = jnp.concatenate(
+        [norm_gain.astype(f32), ffn_gain.astype(f32), segments[0].astype(f32), positions[0].astype(f32)]
+    )
+    smalls = partners(small, "ctx")
+    gains = jnp.stack(reorder([s[: 2 * piece] for s in smalls], c))
+    gains = jnp.stack(partners(gains, "fsdp")).reshape(n_z, n_c, 2, piece)
+    gain_one = gains[:, :, 0].reshape(1, width)
+    gain_two = gains[:, :, 1].reshape(1, width)
+
+    def of_tokens(at):
+        both = [
+            (s[at : at + half], s[at + half : at + token_count]) for s in smalls
+        ]
+        first = [jnp.where(core == 0, a, b) for a, b in both]
+        second = [jnp.where(core == 0, b, a) for a, b in both]
+        return jnp.concatenate(first + second)
+
+    seg_row = of_tokens(2 * piece)
+    pos_row = of_tokens(2 * piece + token_count)
+    place = jnp.arange(half, dtype=jnp.int32)
+    places = jnp.concatenate(
+        [(c ^ kc) * token_count + (core ^ kt) * half + place for kt in range(2) for kc in range(n_c)]
+    )
+
+    out_t = out_weight.T
+    qkv_cols = [
+        jnp.concatenate(parts, axis=1)
+        for parts in zip(
+            split(query_weight, n_c, 1), split(key_weight, n_c, 1), split(value_weight, n_c, 1)
+        )
+    ]
+    qkv_full = partners(jnp.concatenate(exchange(qkv_cols, "ctx"), axis=0), "fsdp")
+    out_full = partners(jnp.concatenate(exchange(split(out_t, n_c, 1), "ctx"), axis=0), "fsdp")
+
+    ffn_cols = [
+        jnp.concatenate(parts, axis=0)
+        for parts in zip(
+            split(gate_weight, n_z, 1), split(up_weight, n_z, 1), split(down_weight.T, n_z, 1)
+        )
+    ]
+    units = ffn_cols[0].shape[1]
+    ffn_mine = [split(b, 3, 0) for b in exchange(ffn_cols, "fsdp")]
+    ffn_mine = jnp.concatenate([b[w] for w in range(3) for b in ffn_mine], axis=0)
+    ffn_full = [split(b, 3, 0) for b in partners(ffn_mine, "ctx")]
+    gate_full = [b[0] for b in ffn_full]
+    up_full = [b[1] for b in ffn_full]
+    down_full = [b[2] for b in ffn_full]
+
+    x_own = plain_to_near(own_half(inputs[0]))
+    x_all = gather_tokens(x_own, "ctx").astype(f32)
+    unit_all, unused = normalize(x_all)
+    normed_one = (unit_all * gain_one).astype(bf16)
+    hidden_own = x_own.astype(f32)
+    unit_one, inverse_one = normalize(hidden_own)
+    qkv = sum_times(normed_one, qkv_full)
+    query_pre, key_pre = qkv[:, : 2 * qk_width], qkv[:, 2 * qk_width : 4 * qk_width]
+    value_rows = qkv[:, 4 * qk_width :].astype(bf16)
+    halfway = qk_width // 2
+    spacing = jnp.arange(halfway, dtype=f32) * (2.0 / qk_width)
+    frequency = jnp.exp(-math.log(rope_base) * spacing)
+    angles = pos_row[:, None] * frequency
+    cos, sin = jnp.cos(angles), jnp.sin(angles)
+    cosine = jnp.concatenate([cos, cos], axis=-1)
+    sine = jnp.concatenate([sin, sin], axis=-1)
+
+    def rotate_maps(v, sines):
+        return jnp.concatenate(
+            [rotate(part, cosine, sines) for part in split(v, 2, 1)], axis=1
+        )
+
+    query_rot = rotate_maps(query_pre, sine).astype(bf16)
+    key_rot = rotate_maps(key_pre, sine).astype(bf16)
+    first_exp = jnp.exp(jnp.sum(lambdas[0] * lambdas[1]))
+    second_exp = jnp.exp(jnp.sum(lambdas[2] * lambdas[3]))
+    weight_lambda = first_exp - second_exp + lambda_init
+    allowed = (seg_row[:, None] == seg_row[None, :]) & (places[None, :] <= places[:, None])
+
+    def shares_of(q, k):
+        masked = jnp.where(allowed, times_t(q, k) * scaling, masked_score)
+        exponent = jnp.where(
+            allowed, jnp.exp(masked - jnp.max(masked, axis=-1, keepdims=True)), 0.0
+        )
+        return exponent / jnp.sum(exponent, axis=-1, keepdims=True)
+
+    queries, keys = split(query_rot, 2, 1), split(key_rot, 2, 1)
+    shares = [shares_of(q, k) for q, k in zip(queries, keys)]
+    mix = (shares[0] - weight_lambda * shares[1]).astype(bf16)
+    attended = times(mix, value_rows)
+    unit_head, inverse_head = normalize(attended)
+    headed = (unit_head * head_gain * (1.0 - lambda_init)).astype(bf16)
+    branch = jnp.concatenate([times_t(headed, b).astype(bf16) for b in out_full], axis=1)
+    middle = hidden_own + scatter_tokens(branch, "ctx")
+
+    def near_to_ffn(v):
+        return plain_to_ffn(plain_to_near(v))
+
+    def ffn_to_near(v):
+        return plain_to_near(ffn_to_plain(v))
+
+    unit_two, inverse_two = normalize(middle)
+    normed_two = gather_tokens(near_to_ffn((unit_two * gain_two).astype(bf16)), "fsdp")
+    grad_own = own_half(cotangent[0])
+    grad_rows = gather_tokens(plain_to_ffn(grad_own), "fsdp")
+    gate_rows = sum_times(normed_two, gate_full)
+    upward = sum_times(normed_two, up_full)
+    sigmoid = jax.nn.sigmoid(gate_rows)
+    hidden_units = (gate_rows * sigmoid * upward).astype(bf16)
+    ffn_out = jnp.concatenate([times_t(hidden_units, b).astype(bf16) for b in down_full], axis=1)
+    result = (plain_to_near(middle) + ffn_to_plain(scatter_tokens(ffn_out, "fsdp"))).astype(bf16)
+
+    hidden_grad = sum_times(grad_rows, down_full)
+    gate_low = (hidden_grad * upward * (sigmoid * (1.0 + gate_rows * (1.0 - sigmoid)))).astype(bf16)
+    up_low = (hidden_grad * (gate_rows * sigmoid)).astype(bf16)
+    two_part = jnp.concatenate(
+        [
+            (times_t(gate_low, g) + times_t(up_low, u)).astype(bf16)
+            for g, u in zip(gate_full, up_full)
+        ],
+        axis=1,
+    )
+    normed_two_grad = ffn_to_near(scatter_tokens(two_part, "fsdp"))
+    gain_two_grad = jnp.sum(normed_two_grad * unit_two, axis=0)
+    middle_grad = plain_to_near(grad_own).astype(f32) + normalize_back(
+        normed_two_grad * gain_two, unit_two, inverse_two
+    )
+    ffn_grads = [
+        jnp.concatenate(
+            [
+                t_times(n, gate_low).astype(bf16),
+                t_times(n, up_low).astype(bf16),
+                t_times(g, hidden_units).astype(bf16),
+            ],
+            axis=0,
+        )
+        for n, g in zip(split(normed_two, n_c, 1), split(grad_rows, n_c, 1))
+    ]
+    ffn_grad = sum_partners(ffn_grads, "ctx").astype(bf16)
+    by_owner = [
+        jnp.concatenate(parts, axis=0)
+        for parts in zip(*[split(g, n_z, 0) for g in split(ffn_grad, 3, 0)])
+    ]
+    arrived = [split(b, 3, 0) for b in exchange(by_owner, "fsdp")]
+    grad_gate, grad_up, grad_down_t = [
+        jnp.concatenate([b[w] for b in arrived], axis=1).astype(f32) for w in range(3)
+    ]
+
+    branch_grad = gather_tokens(middle_grad.astype(bf16), "ctx")
+    headed_grad = sum_times(branch_grad, out_full)
+    scaled_grad = headed_grad * (1.0 - lambda_init)
+    head_gain_grad = jnp.sum(scaled_grad * unit_head, axis=0)
+    attended_grad = normalize_back(scaled_grad * head_gain, unit_head, inverse_head).astype(bf16)
+    mix_grad = times_t(attended_grad, value_rows)
+    first_sum = jnp.sum(shares[0] * mix_grad, axis=-1, keepdims=True)
+    second_sum = jnp.sum(shares[1] * mix_grad, axis=-1, keepdims=True)
+    score_grads = [
+        (shares[0] * (mix_grad - first_sum)).astype(bf16),
+        (-weight_lambda * shares[1] * (mix_grad - second_sum)).astype(bf16),
+    ]
+    value_grad = t_times(mix, attended_grad)
+    query_grad = jnp.concatenate([times(s, k) for s, k in zip(score_grads, keys)], axis=1)
+    key_grad = jnp.concatenate([t_times(s, q) for s, q in zip(score_grads, queries)], axis=1)
+    qkv_low = jnp.concatenate(
+        [
+            rotate_maps(query_grad * scaling, -sine).astype(bf16),
+            rotate_maps(key_grad * scaling, -sine).astype(bf16),
+            value_grad.astype(bf16),
+        ],
+        axis=1,
+    )
+    qkv_grad = sum_partners(
+        [t_times(n, qkv_low).astype(bf16) for n in split(normed_one, n_z, 1)], "fsdp"
+    )
+    out_grad = sum_partners(
+        [t_times(b, headed).astype(bf16) for b in split(branch_grad, n_z, 1)], "fsdp"
+    )
+    qkv_cols = exchange(split(qkv_grad.astype(bf16), n_c, 0), "ctx")
+    out_cols = exchange(split(out_grad.astype(bf16), n_c, 0), "ctx")
+    edges = (0, 2 * qk_width, 4 * qk_width, 4 * qk_width + value_width)
+    grad_query, grad_key, grad_value = [
+        jnp.concatenate([b[:, lo:hi] for b in qkv_cols], axis=1).astype(f32)
+        for lo, hi in zip(edges[:-1], edges[1:])
+    ]
+    grad_out = jnp.concatenate(out_cols, axis=1).astype(f32).T
+    one_part = jnp.concatenate([times_t(qkv_low, b).astype(bf16) for b in qkv_full], axis=1)
+    normed_one_grad = scatter_tokens(one_part, "ctx")
+    gain_one_grad = jnp.sum(normed_one_grad * unit_one, axis=0)
+    grad_own_in = middle_grad + normalize_back(normed_one_grad * gain_one, unit_one, inverse_one)
+    input_grad = plain_to_near(grad_own_in).astype(bf16)
+
+    def both_halves(v):
+        other = partner(v, "tp", 1)
+        return jnp.concatenate(
+            [jnp.where(core == 0, v, other), jnp.where(core == 0, other, v)], axis=0
+        )
+
+    sums = jnp.concatenate(
+        [
+            plain_to_near(gain_one_grad[None])[0],
+            plain_to_near(gain_two_grad[None])[0],
+            head_gain_grad,
+            jnp.full((qk_width,), jnp.sum(second_sum)),
+        ]
+    )
+    for axis in ("tp", "ctx", "fsdp"):
+        bit = 1
+        while bit < lax.axis_size(axis):
+            sums = sums + partner(sums, axis, bit)
+            bit *= 2
+    at = (z * n_c + c) * piece
+    grad_norm_gain = lax.dynamic_slice_in_dim(sums, at, piece)
+    grad_ffn_gain = lax.dynamic_slice_in_dim(sums, width + at, piece)
+    grad_head_gain = sums[2 * width : 2 * width + value_width]
+    lambda_scalar = -sums[2 * width + value_width]
+    grad_lambdas = lambda_scalar * jnp.stack(
+        [
+            first_exp * lambdas[1],
+            first_exp * lambdas[0],
+            -second_exp * lambdas[3],
+            -second_exp * lambdas[2],
+        ]
+    )
+    return (
+        both_halves(result)[None],
+        both_halves(input_grad)[None],
+        grad_norm_gain,
+        grad_query,
+        grad_key,
+        grad_value,
+        grad_out,
+        grad_lambdas,
+        grad_head_gain,
+        grad_ffn_gain,
+        grad_gate,
+        grad_up,
+        grad_down_t.T,
+    )
+
+
 def solution(mesh):
     placed = (
         P("fsdp", "ctx", None),
@@ -399,7 +755,7 @@
         P("fsdp", "ctx", None),
     )
     return jax.shard_map(
-        shards,
+        by_head if fits_by_head(mesh.shape) else shards,
         mesh=mesh,
         in_specs=placed,
         out_specs=(

time: 3130 us -> 852 us (0.27)
  waiting for transfers between devices: 2060 us -> 481 us
  blocking collectives: 566 us -> 0 us
  local copies, waits for them, and re-layouts: 244 us -> 62.9 us
  starting transfers between devices: 7.39 us -> 98.6 us
  matrix products: 179 us -> 93.8 us
  other arithmetic: 39.2 us -> 97.3 us
    reduce_scatter x6 -> x0, waiting for transfers between devices: 1310 us -> none  [the longest x1 483 us: shards(): lax.psum_scatter(grad_down_full, ('fsdp', 'ctx'), scatter_dimension=1, ti...]
    all_gather x9 -> x0, waiting for transfers between devices: 723 us -> none  [the longest x1 174 us: fetch_ffn(): columns = lax.all_gather(down_weight, ('fsdp', 'ctx'), axis=1, tiled=True)]
    ppermute x0 -> x81, waiting for transfers between devices: none -> 481 us  [partner(): lax.ppermute(values, axis, [(i, i ^ step) for i in range(lax.axis_size(ax...]
    unnamed x1 -> x0, blocking collectives: 435 us -> none
    ppermute x0 -> x81, starting transfers between devices: none -> 98.6 us  [partner(): lax.ppermute(values, axis, [(i, i ^ step) for i in range(lax.axis_size(ax...]
    concatenate x4 -> x6, local copies, waits for them, and re-layouts: 99.1 us -> 5.18 us  [the longest x4 4.44 us: gather_tokens(): return jnp.concatenate([near, partner(near, 'tp', 1)], axis=0)]
    dynamic_update_slice x4 -> x0, local copies, waits for them, and re-layouts: 85.4 us -> none  [shards(): lax.scan(grad_step, query_start, blocks)]
    dot_general x40 -> x69, matrix products: 177 us -> 93.8 us  [the longest x23 31.8 us: t_times(): lax.dot_general(left, right, (((0,), (0,)), ((), ())), preferred_element_...]
  transfers between devices with their start and end apart: 19 -> 81, of which waited for: 15 -> 35; matrix products, arithmetic and copies ran while one was open for 9% -> 19% of each run, Pallas kernels for 0% -> 0%
where the time goes in v1:
time: 852 us; the launch traced here: 840 us
  waiting for transfers between devices  481 us (56%)
  starting transfers between devices  98.6 us (12%)
  other arithmetic  97.3 us (11%)
  matrix products  93.8 us (11%)
  local copies, waits for them, and re-layouts  62.9 us (7%)
    ppermute x81, waiting for transfers between devices, partner(): lax.ppermute(values, axis, [(i, i ^ step) for i in range(lax.axis_size(ax...  481 us
    ppermute x81, starting transfers between devices, partner(): lax.ppermute(values, axis, [(i, i ^ step) for i in range(lax.axis_size(ax...  98.6 us
    unnamed x365, local copies, waits for them, and re-layouts  41.6 us
    dot_general x23, matrix products, t_times(): lax.dot_general(left, right, (((0,), (0,)), ((), ())), preferred_element_...  31.8 us
    dot_general x23, matrix products, times(): return jnp.dot(left, right, preferred_element_type=jnp.float32)  31.3 us
    dot_general x23, matrix products, times_t(): lax.dot_general(left, right, (((1,), (1,)), ((), ())), preferred_element_...  30.7 us
  transfers between devices with their start and end apart: 81, of which 35 were waited for; matrix products, arithmetic and copies ran while one was open for 19% of the time, Pallas kernels for 0%

profile of v1, /device:TPU:10, one launch (start us, length us, event | category | flops | bytes accessed | tf_op | source)
XLA Modules:
  0.0 840.3 jit_solution(5719557487725994379)
XLA Ops:
  80.9 8.7 %collective-permute-done.41 = bf16[128,2048]{0,1:T(8,128)(2,1)S(1)} collective-permute-done((bf16[128,2048]{0,1:T(8,128)(2,1)}, bf16[128,2048]{0,1:T(8,128)(2,1)S(1)}, u32[]{:S(2)}, u32[]{:S(2)}) %collective-permute-start.41) | collective-permute-done | bytes 524320 | tf_op jit(solution)/shard_map/ppermute | solution.py:393
  90.7 41.0 %collective-permute-done.42 = bf16[128,2048]{0,1:T(8,128)(2,1)S(1)} collective-permute-done((bf16[128,2048]{0,1:T(8,128)(2,1)}, bf16[128,2048]{0,1:T(8,128)(2,1)S(1)}, u32[]{:S(2)}, u32[]{:S(2)}) %collective-permute-start.42) | collective-permute-done | bytes 524320 | tf_op jit(solution)/shard_map/ppermute | solution.py:393
  133.4 9.7 %collective-permute-done.43 = bf16[128,2048]{0,1:T(8,128)(2,1)S(1)} collective-permute-done((bf16[128,2048]{0,1:T(8,128)(2,1)}, bf16[128,2048]{0,1:T(8,128)(2,1)S(1)}, u32[]{:S(2)}, u32[]{:S(2)}) %collective-permute-start.43) | collective-permute-done | bytes 524320 | tf_op jit(solution)/shard_map/ppermute | solution.py:393
  149.3 10.7 %collective-permute-done.31 = bf16[384,704]{0,1:T(8,128)(2,1)S(1)} collective-permute-done((bf16[384,704]{0,1:T(8,128)(2,1)S(1)}, bf16[384,704]{0,1:T(8,128)(2,1)S(1)}, u32[]{:S(2)}, u32[]{:S(2)}) %collective-permute-start.31) | collective-permute-done | bytes 540704 | tf_op jit(solution)/shard_map/ppermute | solution.py:393
  163.4 14.0 %collective-permute-done.30 = bf16[384,704]{0,1:T(8,128)(2,1)S(1)} collective-permute-done((bf16[384,704]{0,1:T(8,128)(2,1)S(1)}, bf16[384,704]{0,1:T(8,128)(2,1)S(1)}, u32[]{:S(2)}, u32[]{:S(2)}) %collective-permute-start.30) | collective-permute-done | bytes 540704 | tf_op jit(solution)/shard_map/ppermute | solution.py:393
  185.3 53.7 %collective-permute-done.14 = bf16[512,768]{1,0:T(8,128)(2,1)S(1)} collective-permute-done((bf16[512,768]{1,0:T(8,128)(2,1)S(1)}, bf16[512,768]{1,0:T(8,128)(2,1)S(1)}, u32[]{:S(2)}, u32[]{:S(2)}) %collective-permute-start.14) | collective-permute-done | bytes 786464 | tf_op jit(solution)/shard_map/ppermute | solution.py:393
  242.8 13.0 %collective-permute-done.15 = bf16[512,768]{1,0:T(8,128)(2,1)S(1)} collective-permute-done((bf16[512,768]{1,0:T(8,128)(2,1)S(1)}, bf16[512,768]{1,0:T(8,128)(2,1)S(1)}, u32[]{:S(2)}, u32[]{:S(2)}) %collective-permute-start.15) | collective-permute-done | bytes 786464 | tf_op jit(solution)/shard_map/ppermute | solution.py:393
  288.2 8.5 %collective-permute-done.25 = bf16[128,2048]{0,1:T(8,128)(2,1)S(1)} collective-permute-done((bf16[128,2048]{0,1:T(8,128)(2,1)S(1)}, bf16[128,2048]{0,1:T(8,128)(2,1)S(1)}, u32[]{:S(2)}, u32[]{:S(2)}) %collective-permute-start.25) | collective-permute-done | bytes 524320 | tf_op jit(solution)/shard_map/ppermute | solution.py:393
  297.8 9.7 %collective-permute-done.24 = bf16[128,2048]{0,1:T(8,128)(2,1)S(1)} collective-permute-done((bf16[128,2048]{0,1:T(8,128)(2,1)S(1)}, bf16[128,2048]{0,1:T(8,128)(2,1)S(1)}, u32[]{:S(2)}, u32[]{:S(2)}) %collective-permute-start.24) | collective-permute-done | bytes 524320 | tf_op jit(solution)/shard_map/ppermute | solution.py:393
  315.2 17.3 %collective-permute-done.26 = bf16[128,2048]{0,1:T(8,128)(2,1)S(1)} collective-permute-done((bf16[128,2048]{0,1:T(8,128)(2,1)S(1)}, bf16[128,2048]{0,1:T(8,128)(2,1)S(1)}, u32[]{:S(2)}, u32[]{:S(2)}) %collective-permute-start.26) | collective-permute-done | bytes 524320 | tf_op jit(solution)/shard_map/ppermute | solution.py:393
  336.1 13.9 %collective-permute-done.27 = bf16[128,2048]{0,1:T(8,128)(2,1)S(1)} collective-permute-done((bf16[128,2048]{0,1:T(8,128)(2,1)S(1)}, bf16[128,2048]{0,1:T(8,128)(2,1)S(1)}, u32[]{:S(2)}, u32[]{:S(2)}) %collective-permute-start.27) | collective-permute-done | bytes 524320 | tf_op jit(solution)/shard_map/ppermute | solution.py:393
  350.1 10.8 %collective-permute-done.28 = bf16[128,2048]{0,1:T(8,128)(2,1)S(1)} collective-permute-done((bf16[128,2048]{0,1:T(8,128)(2,1)S(1)}, bf16[128,2048]{0,1:T(8,128)(2,1)S(1)}, u32[]{:S(2)}, u32[]{:S(2)}) %collective-permute-start.28) | collective-permute-done | bytes 524320 | tf_op jit(solution)/shard_map/ppermute | solution.py:393
  367.8 32.5 %collective-permute-done.35 = bf16[1536,704]{0,1:T(8,128)(2,1)} collective-permute-done((bf16[1536,704]{0,1:T(8,128)(2,1)}, bf16[1536,704]{0,1:T(8,128)(2,1)}, u32[]{:S(2)}, u32[]{:S(2)}) %collective-permute-start.35) | collective-permute-done | bytes 2162720 | tf_op jit(solution)/shard_map/ppermute | solution.py:393
  418.4 6.2 multiply_convert_fusion.3
  483.9 28.0 %collective-permute-done.77 = bf16[1536,704]{0,1:T(8,128)(2,1)} collective-permute-done((bf16[1536,704]{0,1:T(8,128)(2,1)}, bf16[1536,704]{0,1:T(8,128)(2,1)}, u32[]{:S(2)}, u32[]{:S(2)}) %collective-permute-start.77) | collective-permute-done | bytes 2162720 | tf_op jit(solution)/shard_map/ppermute | solution.py:393
  512.0 45.7 %collective-permute-done.76 = bf16[1536,704]{0,1:T(8,128)(2,1)} collective-permute-done((bf16[1536,704]{0,1:T(8,128)(2,1)S(1)}, bf16[1536,704]{0,1:T(8,128)(2,1)}, u32[]{:S(2)}, u32[]{:S(2)}) %collective-permute-start.76) | collective-permute-done | bytes 2162720 | tf_op jit(solution)/shard_map/ppermute | solution.py:393
  571.7 12.0 %collective-permute-done.39 = bf16[128,2048]{0,1:T(8,128)(2,1)S(1)} collective-permute-done((bf16[128,2048]{0,1:T(8,128)(2,1)S(1)}, bf16[128,2048]{0,1:T(8,128)(2,1)S(1)}, u32[]{:S(2)}, u32[]{:S(2)}) %collective-permute-start.39) | collective-permute-done | bytes 524320 | tf_op jit(solution)/shard_map/ppermute | solution.py:393
  585.5 32.2 %collective-permute-done.38 = bf16[128,2048]{0,1:T(8,128)(2,1)S(1)} collective-permute-done((bf16[128,2048]{0,1:T(8,128)(2,1)S(1)}, bf16[128,2048]{0,1:T(8,128)(2,1)S(1)}, u32[]{:S(2)}, u32[]{:S(2)}) %collective-permute-start.38) | collective-permute-done | bytes 524320 | tf_op jit(solution)/shard_map/ppermute | solution.py:393
  623.7 17.4 %collective-permute-done.50 = bf16[128,2048]{0,1:T(8,128)(2,1)S(1)} collective-permute-done((bf16[128,2048]{0,1:T(8,128)(2,1)S(1)}, bf16[128,2048]{0,1:T(8,128)(2,1)S(1)}, u32[]{:S(2)}, u32[]{:S(2)}) %collective-permute-start.50) | collective-permute-done | bytes 524320 | tf_op jit(solution)/shard_map/ppermute | solution.py:393
  687.4 13.6 %collective-permute-done.71 = bf16[512,256]{0,1:T(8,128)(2,1)S(1)} collective-permute-done((bf16[512,256]{0,1:T(8,128)(2,1)S(1)}, bf16[512,256]{0,1:T(8,128)(2,1)S(1)}, u32[]{:S(2)}, u32[]{:S(2)}) %collective-permute-start.71) | collective-permute-done | bytes 262176 | tf_op jit(solution)/shard_map/ppermute | solution.py:393
  726.5 37.4 %collective-permute-done.65 = bf16[512,768]{1,0:T(8,128)(2,1)} collective-permute-done((bf16[512,768]{1,0:T(8,128)(2,1)}, bf16[512,768]{1,0:T(8,128)(2,1)}, u32[]{:S(2)}, u32[]{:S(2)}) %collective-permute-start.65) | collective-permute-done | bytes 786464 | tf_op jit(solution)/shard_map/ppermute | solution.py:393
  763.9 13.3 %collective-permute-done.64 = bf16[512,768]{1,0:T(8,128)(2,1)} collective-permute-done((bf16[512,768]{1,0:T(8,128)(2,1)}, bf16[512,768]{1,0:T(8,128)(2,1)}, u32[]{:S(2)}, u32[]{:S(2)}) %collective-permute-start.64) | collective-permute-done | bytes 786464 | tf_op jit(solution)/shard_map/ppermute | solution.py:393
  789.7 10.2 %collective-permute-done.67 = bf16[128,768]{1,0:T(8,128)(2,1)S(1)} collective-permute-done((bf16[128,768]{1,0:T(8,128)(2,1)S(1)}, bf16[128,768]{1,0:T(8,128)(2,1)S(1)}, u32[]{:S(2)}, u32[]{:S(2)}) %collective-permute-start.67) | collective-permute-done | bytes 196640 | tf_op jit(solution)/shard_map/ppermute | solution.py:393
  803.5 8.7 %collective-permute-done.55 = bf16[128,2048]{0,1:T(8,128)(2,1)S(1)} collective-permute-done((bf16[128,2048]{0,1:T(8,128)(2,1)S(1)}, bf16[128,2048]{0,1:T(8,128)(2,1)S(1)}, u32[]{:S(2)}, u32[]{:S(2)}) %collective-permute-start.55) | collective-permute-done | bytes 524320 | tf_op jit(solution)/shard_map/ppermute | solution.py:393
  (775 shorter events, 365.8 us)
Async XLA Ops:
  70.3 111.2 %collective-permute-start.6 = (bf16[512,2048]{0,1:T(8,128)(2,1)S(1)}, bf16[512,2048]{0,1:T(8,128)(2,1)S(1)}, u32[]{:S(2)}, u32[]{:S(2)}) collective-permute-start(bf16[512,2048]{0,1:T(8,128)(2,1)S(1)} %pad_maximum_fusion.7), channel_id=1, source_target_pairs={{0,1},{1,0},{2,3},{3,2},{4,5},{5,4},{6,7},{7,6},{8,9},{9,8},{10,11... | collective-permute-start | bytes 6291464 | tf_op jit(solution)/shard_map/ppermute | solution.py:393
  70.4 61.2 %collective-permute-start.42 = (bf16[128,2048]{0,1:T(8,128)(2,1)}, bf16[128,2048]{0,1:T(8,128)(2,1)S(1)}, u32[]{:S(2)}, u32[]{:S(2)}) collective-permute-start(bf16[128,2048]{0,1:T(8,128)(2,1)} %get-tuple-element.200), channel_id=1, source_target_pairs={{0,16},{8,24},{16,0},{24,8},{1,17},{9,25},{17,1},{25,9},{2,18},{10... | collective-permute-start | bytes 1572872 | tf_op jit(solution)/shard_map/ppermute | solution.py:393
  73.4 69.6 %collective-permute-start.43 = (bf16[128,2048]{0,1:T(8,128)(2,1)}, bf16[128,2048]{0,1:T(8,128)(2,1)S(1)}, u32[]{:S(2)}, u32[]{:S(2)}) collective-permute-start(bf16[128,2048]{0,1:T(8,128)(2,1)} %get-tuple-element.200), channel_id=1, source_target_pairs={{0,24},{8,16},{16,8},{24,0},{1,25},{9,17},{17,9},{25,1},{2,26},{10... | collective-permute-start | bytes 1572872 | tf_op jit(solution)/shard_map/ppermute | solution.py:393
  74.4 85.6 %collective-permute-start.31 = (bf16[384,704]{0,1:T(8,128)(2,1)S(1)}, bf16[384,704]{0,1:T(8,128)(2,1)S(1)}, u32[]{:S(2)}, u32[]{:S(2)}) collective-permute-start(bf16[384,704]{0,1:T(8,128)(2,1)S(1)} %copy-done.89), channel_id=1, source_target_pairs={{0,16},{8,24},{16,0},{24,8},{1,17},{9,25},{17,1},{25,9},{2,18},{10... | collective-permute-start | bytes 1622024 | tf_op jit(solution)/shard_map/ppermute | solution.py:393
  89.6 87.8 %collective-permute-start.30 = (bf16[384,704]{0,1:T(8,128)(2,1)S(1)}, bf16[384,704]{0,1:T(8,128)(2,1)S(1)}, u32[]{:S(2)}, u32[]{:S(2)}) collective-permute-start(bf16[384,704]{0,1:T(8,128)(2,1)S(1)} %copy-done.88), channel_id=1, source_target_pairs={{0,24},{8,16},{16,8},{24,0},{1,25},{9,17},{17,9},{25,1},{2,26},{10... | collective-permute-start | bytes 1622024 | tf_op jit(solution)/shard_map/ppermute | solution.py:393
  143.0 125.8 %collective-permute-start.21 = (bf16[512,256]{0,1:T(8,128)(2,1)S(1)}, bf16[512,256]{0,1:T(8,128)(2,1)S(1)}, u32[]{:S(2)}, u32[]{:S(2)}) collective-permute-start(bf16[512,256]{0,1:T(8,128)(2,1)S(1)} %pad_maximum_fusion.30), channel_id=1, source_target_pairs={{0,24},{8,16},{16,8},{24,0},{1,25},{9,17},{17,9},{25,1},{2,26},{10... | collective-permute-start | bytes 786440 | tf_op jit(solution)/shard_map/ppermute | solution.py:393
  160.0 109.4 %collective-permute-start.20 = (bf16[512,256]{0,1:T(8,128)(2,1)S(1)}, bf16[512,256]{0,1:T(8,128)(2,1)S(1)}, u32[]{:S(2)}, u32[]{:S(2)}) collective-permute-start(bf16[512,256]{0,1:T(8,128)(2,1)S(1)} %pad_maximum_fusion.30), channel_id=1, source_target_pairs={{0,16},{8,24},{16,0},{24,8},{1,17},{9,25},{17,1},{25,9},{2,18},{10... | collective-permute-start | bytes 786440 | tf_op jit(solution)/shard_map/ppermute | solution.py:393
  177.4 61.6 %collective-permute-start.14 = (bf16[512,768]{1,0:T(8,128)(2,1)S(1)}, bf16[512,768]{1,0:T(8,128)(2,1)S(1)}, u32[]{:S(2)}, u32[]{:S(2)}) collective-permute-start(bf16[512,768]{1,0:T(8,128)(2,1)S(1)} %pad_maximum_fusion.12), channel_id=1, source_target_pairs={{0,16},{8,24},{16,0},{24,8},{1,17},{9,25},{17,1},{25,9},{2,18},{10... | collective-permute-start | bytes 2359304 | tf_op jit(solution)/shard_map/ppermute | solution.py:393
  177.4 64.3 %collective-permute-start.13 = (bf16[512,768]{1,0:T(8,128)(2,1)S(1)}, bf16[512,768]{1,0:T(8,128)(2,1)S(1)}, u32[]{:S(2)}, u32[]{:S(2)}) collective-permute-start(bf16[512,768]{1,0:T(8,128)(2,1)S(1)} %pad_maximum_fusion.12), channel_id=1, source_target_pairs={{0,8},{8,0},{16,24},{24,16},{1,9},{9,1},{17,25},{25,17},{2,10},{10... | collective-permute-start | bytes 2359304 | tf_op jit(solution)/shard_map/ppermute | solution.py:393
  181.5 74.3 %collective-permute-start.15 = (bf16[512,768]{1,0:T(8,128)(2,1)S(1)}, bf16[512,768]{1,0:T(8,128)(2,1)S(1)}, u32[]{:S(2)}, u32[]{:S(2)}) collective-permute-start(bf16[512,768]{1,0:T(8,128)(2,1)S(1)} %pad_maximum_fusion.12), channel_id=1, source_target_pairs={{0,24},{8,16},{16,8},{24,0},{1,25},{9,17},{17,9},{25,1},{2,26},{10... | collective-permute-start | bytes 2359304 | tf_op jit(solution)/shard_map/ppermute | solution.py:393
  241.7 71.5 %collective-permute-start.44 = (bf16[512,2048]{0,1:T(8,128)(2,1)S(1)}, bf16[512,2048]{0,1:T(8,128)(2,1)}, u32[]{:S(2)}, u32[]{:S(2)}) collective-permute-start(bf16[512,2048]{0,1:T(8,128)(2,1)S(1)} %pad_maximum_fusion.9), channel_id=1, source_target_pairs={{0,1},{1,0},{2,3},{3,2},{4,5},{5,4},{6,7},{7,6},{8,9},{9,8},{10,11... | collective-permute-start | bytes 6291464 | tf_op jit(solution)/shard_map/ppermute | solution.py:393
  286.7 79.3 %collective-permute-start.34 = (bf16[1536,704]{0,1:T(8,128)(2,1)}, bf16[1536,704]{0,1:T(8,128)(2,1)S(1)}, u32[]{:S(2)}, u32[]{:S(2)}) collective-permute-start(bf16[1536,704]{0,1:T(8,128)(2,1)} %constant_dynamic-update-slice_fusion.13), channel_id=1, source_target_pairs={{0,4},{2,6},{4,0},{6,2},{1,5},{3,7},{5,1},{7,3},{8,12},{10,14},{12... | collective-permute-start | bytes 6488072 | tf_op jit(solution)/shard_map/ppermute | solution.py:393
  296.7 70.2 %collective-permute-start.33 = (bf16[1536,704]{0,1:T(8,128)(2,1)}, bf16[1536,704]{0,1:T(8,128)(2,1)S(1)}, u32[]{:S(2)}, u32[]{:S(2)}) collective-permute-start(bf16[1536,704]{0,1:T(8,128)(2,1)} %constant_dynamic-update-slice_fusion.13), channel_id=1, source_target_pairs={{0,2},{2,0},{4,6},{6,4},{1,3},{3,1},{5,7},{7,5},{8,10},{10,8},{12,... | collective-permute-start | bytes 6488072 | tf_op jit(solution)/shard_map/ppermute | solution.py:393
  307.5 92.8 %collective-permute-start.35 = (bf16[1536,704]{0,1:T(8,128)(2,1)}, bf16[1536,704]{0,1:T(8,128)(2,1)}, u32[]{:S(2)}, u32[]{:S(2)}) collective-permute-start(bf16[1536,704]{0,1:T(8,128)(2,1)} %constant_dynamic-update-slice_fusion.13), channel_id=1, source_target_pairs={{0,6},{2,4},{4,2},{6,0},{1,7},{3,5},{5,3},{7,1},{8,14},{10,12},{12... | collective-permute-start | bytes 6488072 | tf_op jit(solution)/shard_map/ppermute | solution.py:393
  462.5 95.1 %collective-permute-start.76 = (bf16[1536,704]{0,1:T(8,128)(2,1)S(1)}, bf16[1536,704]{0,1:T(8,128)(2,1)}, u32[]{:S(2)}, u32[]{:S(2)}) collective-permute-start(bf16[1536,704]{0,1:T(8,128)(2,1)S(1)} %pad_maximum_fusion.5), channel_id=1, source_target_pairs={{0,4},{2,6},{4,0},{6,2},{1,5},{3,7},{5,1},{7,3},{8,12},{10,14},{12... | collective-permute-start | bytes 6488072 | tf_op jit(solution)/shard_map/ppermute | solution.py:393
  469.8 90.0 %collective-permute-start.75 = (bf16[1536,704]{0,1:T(8,128)(2,1)}, bf16[1536,704]{0,1:T(8,128)(2,1)}, u32[]{:S(2)}, u32[]{:S(2)}) collective-permute-start(bf16[1536,704]{0,1:T(8,128)(2,1)} %pad_maximum_fusion.4), channel_id=1, source_target_pairs={{0,2},{2,0},{4,6},{6,4},{1,3},{3,1},{5,7},{7,5},{8,10},{10,8},{12,... | collective-permute-start | bytes 6488072 | tf_op jit(solution)/shard_map/ppermute | solution.py:393
  477.7 87.2 %collective-permute-start.48 = (bf16[128,2048]{0,1:T(8,128)(2,1)S(1)}, bf16[128,2048]{0,1:T(8,128)(2,1)S(1)}, u32[]{:S(2)}, u32[]{:S(2)}) collective-permute-start(bf16[128,2048]{0,1:T(8,128)(2,1)S(1)} %get-tuple-element.107), channel_id=1, source_target_pairs={{0,24},{8,16},{16,8},{24,0},{1,25},{9,17},{17,9},{25,1},{2,26},{10... | collective-permute-start | bytes 1572872 | tf_op jit(solution)/shard_map/ppermute | solution.py:393
  481.2 85.3 %collective-permute-start.47 = (bf16[128,2048]{0,1:T(8,128)(2,1)S(1)}, bf16[128,2048]{0,1:T(8,128)(2,1)S(1)}, u32[]{:S(2)}, u32[]{:S(2)}) collective-permute-start(bf16[128,2048]{0,1:T(8,128)(2,1)S(1)} %get-tuple-element.108), channel_id=1, source_target_pairs={{0,16},{8,24},{16,0},{24,8},{1,17},{9,25},{17,1},{25,9},{2,18},{10... | collective-permute-start | bytes 1572872 | tf_op jit(solution)/shard_map/ppermute | solution.py:393
  566.5 74.9 %collective-permute-start.78 = (bf16[384,704]{0,1:T(8,128)(2,1)S(1)}, bf16[384,704]{0,1:T(8,128)(2,1)S(1)}, u32[]{:S(2)}, u32[]{:S(2)}) collective-permute-start(bf16[384,704]{0,1:T(8,128)(2,1)S(1)} %broadcast_select_fusion.23), channel_id=1, source_target_pairs={{0,24},{8,16},{16,8},{24,0},{1,25},{9,17},{17,9},{25,1},{2,26},{10... | collective-permute-start | bytes 1622024 | tf_op jit(solution)/shard_map/ppermute | solution.py:393
  568.5 72.9 %collective-permute-start.79 = (bf16[384,704]{0,1:T(8,128)(2,1)S(1)}, bf16[384,704]{0,1:T(8,128)(2,1)S(1)}, u32[]{:S(2)}, u32[]{:S(2)}) collective-permute-start(bf16[384,704]{0,1:T(8,128)(2,1)S(1)} %get-tuple-element.41), channel_id=1, source_target_pairs={{0,16},{8,24},{16,0},{24,8},{1,17},{9,25},{17,1},{25,9},{2,18},{10... | collective-permute-start | bytes 1622024 | tf_op jit(solution)/shard_map/ppermute | solution.py:393
  680.6 102.2 %collective-permute-start.53 = (bf16[512,2048]{0,1:T(8,128)(2,1)}, bf16[512,2048]{0,1:T(8,128)(2,1)}, u32[]{:S(2)}, u32[]{:S(2)}) collective-permute-start(bf16[512,2048]{0,1:T(8,128)(2,1)} %slice.390), channel_id=1, source_target_pairs={{0,1},{1,0},{2,3},{3,2},{4,5},{5,4},{6,7},{7,6},{8,9},{9,8},{10,11... | collective-permute-start | bytes 6291464 | tf_op jit(solution)/shard_map/ppermute | solution.py:393
  709.9 67.3 %collective-permute-start.64 = (bf16[512,768]{1,0:T(8,128)(2,1)}, bf16[512,768]{1,0:T(8,128)(2,1)}, u32[]{:S(2)}, u32[]{:S(2)}) collective-permute-start(bf16[512,768]{1,0:T(8,128)(2,1)} %convolution_convert_fusion.13), channel_id=1, source_target_pairs={{0,16},{8,24},{16,0},{24,8},{1,17},{9,25},{17,1},{25,9},{2,18},{10... | collective-permute-start | bytes 2359304 | tf_op jit(solution)/shard_map/ppermute | solution.py:393
  714.2 63.0 %collective-permute-start.63 = (bf16[512,768]{1,0:T(8,128)(2,1)}, bf16[512,768]{1,0:T(8,128)(2,1)}, u32[]{:S(2)}, u32[]{:S(2)}) collective-permute-start(bf16[512,768]{1,0:T(8,128)(2,1)} %convolution_convert_fusion.14), channel_id=1, source_target_pairs={{0,8},{8,0},{16,24},{24,16},{1,9},{9,1},{17,25},{25,17},{2,10},{10... | collective-permute-start | bytes 2359304 | tf_op jit(solution)/shard_map/ppermute | solution.py:393
  725.6 109.9 %collective-permute-start.40 = (bf16[128,2048]{0,1:T(8,128)(2,1)S(1)}, bf16[128,2048]{0,1:T(8,128)(2,1)S(1)}, u32[]{:S(2)}, u32[]{:S(2)}) collective-permute-start(bf16[128,2048]{0,1:T(8,128)(2,1)S(1)} %fusion.27), channel_id=1, source_target_pairs={{0,1},{1,0},{2,3},{3,2},{4,5},{5,4},{6,7},{7,6},{8,9},{9,8},{10,11... | collective-permute-start | bytes 1572872 | tf_op jit(solution)/shard_map/ppermute | solution.py:393
  (216 other events, 4941.3 us)
